TPU v7x, 256 devices: a whole 4x4x8 slice. The times are simulated.
256 devices in a mesh: row: 32 (over x, y, core), col: 8 (over z).
Axes of the slice: x: 4, y: 4, z: 8, core: 2. Of those that a mesh axis runs over, the one named last changes fastest.
Arguments:
- source: bfloat16 [32768, 128], P(('row', 'col')), may hold values from -10 to 10
- target: bfloat16 [32768, 128], P(('col', 'row')), may hold values from -80 to 80
- target_potential: bfloat16 [32768], P(('col', 'row')), may hold values from -4 to 4
- prev_moment: float32 [128, 128], replicated, may hold values from -0.1 to 0.5
Outputs:
- moment: float32 [128, 128], replicated
- source_potential: float32 [32768], P('row')
- target_update: float32 [32768], P(('col', 'row'))
All inputs are finite; a program needn't handle non-finite values.
Results may differ from a plain program's by a relative error of at most 0.0059.
Values may be sent and summed in bfloat16 or wider, within the bound.
A program may use at most 64 MiB of HBM per device.

v0:
```python
import math
import jax
import jax.numpy as jnp
from jax import lax
from jax.sharding import PartitionSpec as P

ITERS = 2


def project(rows_block, matrix):
    return jnp.dot(rows_block.astype(jnp.float32), matrix, precision=lax.Precision.HIGHEST).astype(
        jnp.bfloat16
    )


def tile_costs(projected, cols_block):
    return -4.0 * lax.dot_general(
        projected, cols_block, (((1,), (1,)), ((), ())), preferred_element_type=jnp.float32
    )


def row_totals(scores):
    top_score = lax.pmax(jnp.max(scores, axis=1), "col")
    mass_total = lax.psum(jnp.sum(jnp.exp(scores - top_score[:, None]), axis=1), "col")
    return top_score + jnp.log(mass_total)


def column_totals(scores):
    top_score = lax.pmax(jnp.max(scores, axis=0), "row")
    mass_total = lax.psum(jnp.sum(jnp.exp(scores - top_score[None, :]), axis=0), "row")
    return top_score + jnp.log(mass_total)


def per_device(source, target, target_potential, prev_moment):
    rows_block = lax.all_gather(source, "col", axis=0, tiled=True)
    cols_block, potential = (
        lax.all_gather(target, "row", axis=0, tiled=True),
        lax.all_gather(target_potential, "row", axis=0, tiled=True),
    )
    row_devices = lax.axis_size("row")
    rows_total = rows_block.shape[0] * row_devices
    cols_total = cols_block.shape[0] * lax.axis_size("col")
    share_width = cols_block.shape[0] // row_devices
    position = lax.axis_index("row")
    column = potential.astype(jnp.float32)
    scores = column[None, :] - tile_costs(project(rows_block, prev_moment), cols_block)
    spread = row_totals(scores)
    weights = (jnp.exp(scores - spread[:, None]) / rows_total).astype(jnp.bfloat16)
    carried = jnp.dot(weights, cols_block, preferred_element_type=jnp.float32)
    partial_moment = lax.dot_general(
        rows_block.astype(jnp.float32),
        carried,
        (((0,), (0,)), ((), ())),
        precision=lax.Precision.HIGHEST,
    )
    moment = lax.psum(partial_moment, ("row", "col"))
    cost_tile = tile_costs(project(rows_block, moment), cols_block)
    source_potential = jnp.zeros((rows_block.shape[0],), jnp.float32)
    own_share = jnp.zeros((share_width,), jnp.float32)
    for iteration in range(ITERS):
        source_potential = math.log(cols_total) - row_totals(column[None, :] - cost_tile)
        column_scores = source_potential[:, None] - cost_tile
        column = math.log(rows_total) - column_totals(column_scores)
        own_share = lax.dynamic_slice_in_dim(column, position * share_width, share_width)
    return (moment, source_potential, own_share)


def solution(mesh):
    placed = (P(("row", "col"), None), P(("col", "row"), None), P(("col", "row")), P())
    return jax.shard_map(
        per_device,
        mesh=mesh,
        in_specs=placed,
        out_specs=(P(), P("row"), P(("col", "row"))),
        check_vma=False,
    )
```

profile of v0, /device:TPU:32, one launch (start us, length us, event | category | flops | bytes accessed | tf_op | source)
XLA Modules:
  0.0 979.2 jit_solution(412638877074749381)
XLA Ops:
  8.0 21.8 %all-gather = bf16[32,1,128]{2,1,0:T(2,128)(2,1)S(1)} all-gather(bf16[1,1,128]{2,1,0:T(2,128)(2,1)} %bitcast.20), channel_id=1, replica_groups=mesh['row'=32,'col'=8] {'row'}, dimensions={0}, use_global_device_ids=true | all-gather | bytes 8448 | tf_op jit(solution)/shard_map/all_gather | solution.py:38
  29.8 27.7 %all_gather.10 = bf16[1024,128]{1,0:T(8,128)(2,1)S(1)} all-gather(bf16[128,128]{1,0:T(8,128)(2,1)} %param.4), channel_id=1, replica_groups=mesh['row'=32,'col'=8] {'col'}, dimensions={0}, use_global_device_ids=true | all-gather | bytes 294912 | tf_op jit(solution)/shard_map/all_gather | solution.py:35
  61.0 8.3 fusion
  69.3 16.0 %pmax.35 = f32[1024]{0:T(1024)S(1)} all-reduce(f32[1024]{0:T(1024)S(1)} %get-tuple-element.9), channel_id=1, replica_groups=mesh['row'=32,'col'=8] {'col'}, use_global_device_ids=true, to_apply=%region_1.0 | all-reduce | flops 1024 | bytes 8192 | tf_op jit(solution)/shard_map/pmax | solution.py:23
  85.4 7.8 exponential_reduce_fusion.4
  93.2 16.0 %psum.42 = f32[1024]{0:T(1024)S(1)} all-reduce(f32[1024]{0:T(1024)S(1)} %exponential_reduce_fusion.4), channel_id=1, replica_groups=mesh['row'=32,'col'=8] {'col'}, use_global_device_ids=true, to_apply=%region_3.0 | all-reduce | flops 1024 | bytes 8192 | tf_op jit(solution)/shard_map/psum | solution.py:24
  109.2 7.8 fusion.1
  118.3 234.4 %all-reduce.2.cloned.1.call-done = f32[128,128]{0,1:T(8,128)} async-done(((f32[128,128]{0,1:T(8,128)}), f32[128,128]{0,1:T(8,128)}) %all-reduce.2.cloned.1.call-update) | async-done | bytes 65552 | tf_op jit(solution)/shard_map/psum | solution.py:56
  353.9 7.0 subtract_reduce_fusion.3
  360.9 15.2 %pmax.36 = f32[1024]{0:T(1024)S(1)} all-reduce(f32[1024]{0:T(1024)S(1)} %get-tuple-element.11), channel_id=1, replica_groups=mesh['row'=32,'col'=8] {'col'}, use_global_device_ids=true, to_apply=%region_6.0 | all-reduce | flops 1024 | bytes 8192 | tf_op jit(solution)/shard_map/pmax | solution.py:23
  376.1 7.8 exponential_reduce_fusion.3
  384.0 15.1 %psum.44 = f32[1024]{0:T(1024)S(1)} all-reduce(f32[1024]{0:T(1024)S(1)} %exponential_reduce_fusion.3), channel_id=1, replica_groups=mesh['row'=32,'col'=8] {'col'}, use_global_device_ids=true, to_apply=%region_8.0 | all-reduce | flops 1024 | bytes 8192 | tf_op jit(solution)/shard_map/psum | solution.py:24
  399.1 7.7 subtract_reduce_fusion.2
  406.8 124.0 %pmax.37 = f32[4096]{0:T(1024)S(1)} all-reduce(f32[4096]{0:T(1024)S(1)} %subtract_reduce_fusion.2), channel_id=1, replica_groups=mesh['row'=32,'col'=8] {'row'}, use_global_device_ids=true, to_apply=%region_10.0 | all-reduce | flops 4096 | bytes 32768 | tf_op jit(solution)/shard_map/pmax | solution.py:29
  530.8 7.7 exponential_reduce_fusion.2
  538.5 123.8 %psum.45 = f32[4096]{0:T(1024)S(1)} all-reduce(f32[4096]{0:T(1024)S(1)} %exponential_reduce_fusion.2), channel_id=1, replica_groups=mesh['row'=32,'col'=8] {'row'}, use_global_device_ids=true, to_apply=%region_12.0 | all-reduce | flops 4096 | bytes 32768 | tf_op jit(solution)/shard_map/psum | solution.py:30
  662.3 7.5 subtract_reduce_fusion.1
  669.8 15.2 %pmax.38 = f32[1024]{0:T(1024)S(1)} all-reduce(f32[1024]{0:T(1024)S(1)} %subtract_reduce_fusion.1), channel_id=1, replica_groups=mesh['row'=32,'col'=8] {'col'}, use_global_device_ids=true, to_apply=%region_14.0 | all-reduce | flops 1024 | bytes 8192 | tf_op jit(solution)/shard_map/pmax | solution.py:23
  685.0 7.8 exponential_reduce_fusion.1
  692.8 15.1 %psum.46 = f32[1024]{0:T(1024)S(1)} all-reduce(f32[1024]{0:T(1024)S(1)} %exponential_reduce_fusion.1), channel_id=1, replica_groups=mesh['row'=32,'col'=8] {'col'}, use_global_device_ids=true, to_apply=%region_16.0 | all-reduce | flops 1024 | bytes 8192 | tf_op jit(solution)/shard_map/psum | solution.py:24
  708.0 7.8 subtract_reduce_fusion
  715.7 123.8 %pmax.39 = f32[4096]{0:T(1024)S(1)} all-reduce(f32[4096]{0:T(1024)S(1)} %subtract_reduce_fusion), channel_id=1, replica_groups=mesh['row'=32,'col'=8] {'row'}, use_global_device_ids=true, to_apply=%region_18.0 | all-reduce | flops 4096 | bytes 32768 | tf_op jit(solution)/shard_map/pmax | solution.py:29
  839.5 7.7 exponential_reduce_fusion
  847.3 123.8 %psum.47 = f32[4096]{0:T(1024)S(1)} all-reduce(f32[4096]{0:T(1024)S(1)} %exponential_reduce_fusion), channel_id=1, replica_groups=mesh['row'=32,'col'=8] {'row'}, use_global_device_ids=true, to_apply=%region_20.0 | all-reduce | flops 4096 | bytes 32768 | tf_op jit(solution)/shard_map/psum | solution.py:30
  (23 shorter events, 8.1 us)
Async XLA Ops:
  7.2 50.3 %copy-start = (f32[128,128]{1,0:T(8,128)S(1)}, f32[128,128]{1,0:T(8,128)}, u32[]{:S(2)}) copy-start(f32[128,128]{1,0:T(8,128)} %param.7) | copy-start | bytes 196612
  7.2 53.8 %all-gather.3.cloned.1.call-start = ((), (), s32[]{:S(2)}) async-start(), calls=%async_computation | async-start | bytes 1081344 | tf_op jit(solution)/shard_map/all_gather | solution.py:37
  7.9 344.7 %all-reduce.2.cloned.1.call-start = ((), (), s32[]{:S(2)}) async-start(), calls=%async_computation.1 | async-start | bytes 131072 | tf_op jit(solution)/shard_map/psum | solution.py:56
  61.0 48.2 %copy-start.1 = (bf16[4096,128]{1,0:T(8,128)(2,1)S(1)}, bf16[4096,128]{1,0:T(8,128)(2,1)}, u32[]{:S(2)}) copy-start(bf16[4096,128]{1,0:T(8,128)(2,1)} %all-gather.3.cloned.1.call-done) | copy-start | bytes 3145732
  708.0 139.3 %copy-start.3 = (f32[1024]{0:T(1024)}, f32[1024]{0:T(1024)S(1)}, u32[]{:S(2)}) copy-start(f32[1024]{0:T(1024)S(1)} %add_subtract_fusion.1) | copy-start | bytes 12292
  708.0 263.7 %copy-start.2 = (f32[128,128]{0,1:T(8,128)S(1)}, f32[128,128]{0,1:T(8,128)}, u32[]{:S(2)}) copy-start(f32[128,128]{0,1:T(8,128)} %all-reduce.2.cloned.1.call-done) | copy-start | bytes 196612
Sparse Core Ops, SparseCore 0:
  10.6 50.3 all-gather.2
  118.4 234.2 all-reduce.1
where the time goes:
time: 980 us; the launch traced here: 979 us
  blocking collectives  638 us (65%)
  waiting for transfers between devices  238 us (24%)
  other arithmetic  62.6 us (6%)
  matrix products  25.9 us (3%)
  between operations  14.1 us (1%)
    pmax x2, blocking collectives, column_totals(): top_score = lax.pmax(jnp.max(scores, axis=0), 'row')  248 us
    psum x2, blocking collectives, column_totals(): lax.psum(jnp.sum(jnp.exp(scores - top_score[None, :]), axis=0), 'row')  248 us
    psum x1, waiting for transfers between devices, per_device(): moment = lax.psum(partial_moment, ('row', 'col'))  234 us
    pmax x3, blocking collectives, row_totals(): top_score = lax.pmax(jnp.max(scores, axis=1), 'col')  46.5 us
    psum x3, blocking collectives, row_totals(): lax.psum(jnp.sum(jnp.exp(scores - top_score[:, None]), axis=1), 'col')  46.2 us
    all_gather x1, blocking collectives, per_device(): rows_block = lax.all_gather(source, 'col', axis=0, tiled=True)  27.7 us
    reduce_sum x3, other arithmetic, row_totals(): jnp.sum(jnp.exp(scores - top_score[:, None]), axis=1)  23.5 us
    all_gather x1, blocking collectives, per_device(): lax.all_gather(target_potential, 'row', axis=0, tiled=True)  21.8 us
  transfers between devices with their start and end apart: 2, of which 2 were waited for; matrix products, arithmetic and copies ran while one was open for 0% of the time, Pallas kernels for 0%

commit v1 on v0

--- a/solution.py
+++ b/solution.py
@@ -5,6 +5,12 @@
 from jax.sharding import PartitionSpec as P
 
 ITERS = 2
+
+
+def advance_orders(block_here):
+    for s in ("col", "row"):
+        block_here = lax.psum(block_here, s)
+    return block_here
 
 
 def project(rows_block, matrix):
@@ -53,7 +59,7 @@
         (((0,), (0,)), ((), ())),
         precision=lax.Precision.HIGHEST,
     )
-    moment = lax.psum(partial_moment, ("row", "col"))
+    moment = advance_orders(partial_moment)
     cost_tile = tile_costs(project(rows_block, moment), cols_block)
     source_potential = jnp.zeros((rows_block.shape[0],), jnp.float32)
     own_share = jnp.zeros((share_width,), jnp.float32)

time: 980 us -> 924 us (0.943)
  waiting for transfers between devices: 238 us -> 181 us
    psum x1 -> x2, waiting for transfers between devices: 234 us -> 177 us  [advance_orders(): block_here = lax.psum(block_here, s)]
  transfers between devices with their start and end apart: 2 -> 3, of which waited for: 2 -> 3; matrix products, arithmetic and copies ran while one was open for 0% -> 0% of each run, Pallas kernels for 0% -> 0%
where the time goes in v1:
time: 924 us; the launch traced here: 923 us
  blocking collectives  639 us (69%)
  waiting for transfers between devices  181 us (20%)
  other arithmetic  62.6 us (7%)
  matrix products  25.9 us (3%)
  between operations  13.8 us (1%)
    pmax x2, blocking collectives, column_totals(): top_score = lax.pmax(jnp.max(scores, axis=0), 'row')  248 us
    psum x2, blocking collectives, column_totals(): lax.psum(jnp.sum(jnp.exp(scores - top_score[None, :]), axis=0), 'row')  248 us
    psum x2, waiting for transfers between devices, advance_orders(): block_here = lax.psum(block_here, s)  177 us
    psum x3, blocking collectives, row_totals(): lax.psum(jnp.sum(jnp.exp(scores - top_score[:, None]), axis=1), 'col')  47.3 us
    pmax x3, blocking collectives, row_totals(): top_score = lax.pmax(jnp.max(scores, axis=1), 'col')  47.1 us
    all_gather x1, blocking collectives, per_device(): rows_block = lax.all_gather(source, 'col', axis=0, tiled=True)  27.7 us
    reduce_sum x3, other arithmetic, row_totals(): jnp.sum(jnp.exp(scores - top_score[:, None]), axis=1)  23.5 us
    all_gather x1, blocking collectives, per_device(): lax.all_gather(target_potential, 'row', axis=0, tiled=True)  21.8 us
  transfers between devices with their start and end apart: 3, of which 3 were waited for; matrix products, arithmetic and copies ran while one was open for 0% of the time, Pallas kernels for 0%

profile of v1, /device:TPU:32, one launch (start us, length us, event | category | flops | bytes accessed | tf_op | source)
XLA Modules:
  0.0 923.3 jit_solution(5181491558607512836)
XLA Ops:
  8.0 21.8 %all-gather = bf16[32,1,128]{2,1,0:T(2,128)(2,1)S(1)} all-gather(bf16[1,1,128]{2,1,0:T(2,128)(2,1)} %bitcast.20), channel_id=1, replica_groups=mesh['row'=32,'col'=8] {'row'}, dimensions={0}, use_global_device_ids=true | all-gather | bytes 8448 | tf_op jit(solution)/shard_map/all_gather | solution.py:44
  29.8 27.7 %all_gather.10 = bf16[1024,128]{1,0:T(8,128)(2,1)S(1)} all-gather(bf16[128,128]{1,0:T(8,128)(2,1)} %param.4), channel_id=1, replica_groups=mesh['row'=32,'col'=8] {'col'}, dimensions={0}, use_global_device_ids=true | all-gather | bytes 294912 | tf_op jit(solution)/shard_map/all_gather | solution.py:41
  61.0 8.3 fusion
  69.3 16.0 %pmax.35 = f32[1024]{0:T(1024)S(1)} all-reduce(f32[1024]{0:T(1024)S(1)} %get-tuple-element.9), channel_id=1, replica_groups=mesh['row'=32,'col'=8] {'col'}, use_global_device_ids=true, to_apply=%region_1.0 | all-reduce | flops 1024 | bytes 8192 | tf_op jit(solution)/shard_map/pmax | solution.py:29
  85.4 7.8 exponential_reduce_fusion.4
  93.2 16.0 %psum.49 = f32[1024]{0:T(1024)S(1)} all-reduce(f32[1024]{0:T(1024)S(1)} %exponential_reduce_fusion.4), channel_id=1, replica_groups=mesh['row'=32,'col'=8] {'col'}, use_global_device_ids=true, to_apply=%region_3.0 | all-reduce | flops 1024 | bytes 8192 | tf_op jit(solution)/shard_map/psum | solution.py:30
  109.2 7.8 fusion.1
  118.3 68.9 %all-reduce.3.cloned.1.call-done = f32[128,128]{0,1:T(8,128)} async-done(((f32[128,128]{0,1:T(8,128)}), f32[128,128]{0,1:T(8,128)}) %all-reduce.3.cloned.1.call-update) | async-done | bytes 65552 | tf_op jit(solution)/shard_map/psum | solution.py:12
  187.2 108.0 %all-reduce.5.cloned.1.call-done = f32[128,128]{0,1:T(8,128)} async-done(((f32[128,128]{0,1:T(8,128)}), f32[128,128]{0,1:T(8,128)}) %all-reduce.5.cloned.1.call-update) | async-done | bytes 65552 | tf_op jit(solution)/shard_map/psum | solution.py:12
  303.5 16.1 %pmax.36 = f32[1024]{0:T(1024)S(1)} all-reduce(f32[1024]{0:T(1024)S(1)} %get-tuple-element.11), channel_id=1, replica_groups=mesh['row'=32,'col'=8] {'col'}, use_global_device_ids=true, to_apply=%region_7.0 | all-reduce | flops 1024 | bytes 8192 | tf_op jit(solution)/shard_map/pmax | solution.py:29
  319.6 7.8 exponential_reduce_fusion.3
  327.4 16.0 %psum.52 = f32[1024]{0:T(1024)S(1)} all-reduce(f32[1024]{0:T(1024)S(1)} %exponential_reduce_fusion.3), channel_id=1, replica_groups=mesh['row'=32,'col'=8] {'col'}, use_global_device_ids=true, to_apply=%region_9.0 | all-reduce | flops 1024 | bytes 8192 | tf_op jit(solution)/shard_map/psum | solution.py:30
  343.4 7.7 subtract_reduce_fusion.2
  351.2 124.0 %pmax.37 = f32[4096]{0:T(1024)S(1)} all-reduce(f32[4096]{0:T(1024)S(1)} %subtract_reduce_fusion.2), channel_id=1, replica_groups=mesh['row'=32,'col'=8] {'row'}, use_global_device_ids=true, to_apply=%region_11.0 | all-reduce | flops 4096 | bytes 32768 | tf_op jit(solution)/shard_map/pmax | solution.py:35
  475.1 7.7 exponential_reduce_fusion.2
  482.9 123.8 %psum.53 = f32[4096]{0:T(1024)S(1)} all-reduce(f32[4096]{0:T(1024)S(1)} %exponential_reduce_fusion.2), channel_id=1, replica_groups=mesh['row'=32,'col'=8] {'row'}, use_global_device_ids=true, to_apply=%region_13.0 | all-reduce | flops 4096 | bytes 32768 | tf_op jit(solution)/shard_map/psum | solution.py:36
  606.7 7.5 subtract_reduce_fusion.1
  614.1 15.0 %pmax.38 = f32[1024]{0:T(1024)S(1)} all-reduce(f32[1024]{0:T(1024)S(1)} %subtract_reduce_fusion.1), channel_id=1, replica_groups=mesh['row'=32,'col'=8] {'col'}, use_global_device_ids=true, to_apply=%region_15.0 | all-reduce | flops 1024 | bytes 8192 | tf_op jit(solution)/shard_map/pmax | solution.py:29
  629.2 7.8 exponential_reduce_fusion.1
  637.0 15.3 %psum.54 = f32[1024]{0:T(1024)S(1)} all-reduce(f32[1024]{0:T(1024)S(1)} %exponential_reduce_fusion.1), channel_id=1, replica_groups=mesh['row'=32,'col'=8] {'col'}, use_global_device_ids=true, to_apply=%region_17.0 | all-reduce | flops 1024 | bytes 8192 | tf_op jit(solution)/shard_map/psum | solution.py:30
  652.3 7.8 subtract_reduce_fusion
  660.1 123.8 %pmax.39 = f32[4096]{0:T(1024)S(1)} all-reduce(f32[4096]{0:T(1024)S(1)} %subtract_reduce_fusion), channel_id=1, replica_groups=mesh['row'=32,'col'=8] {'row'}, use_global_device_ids=true, to_apply=%region_19.0 | all-reduce | flops 4096 | bytes 32768 | tf_op jit(solution)/shard_map/pmax | solution.py:35
  783.9 7.7 exponential_reduce_fusion
  791.6 123.8 %psum.55 = f32[4096]{0:T(1024)S(1)} all-reduce(f32[4096]{0:T(1024)S(1)} %exponential_reduce_fusion), channel_id=1, replica_groups=mesh['row'=32,'col'=8] {'row'}, use_global_device_ids=true, to_apply=%region_21.0 | all-reduce | flops 4096 | bytes 32768 | tf_op jit(solution)/shard_map/psum | solution.py:36
  (26 shorter events, 15.2 us)
Async XLA Ops:
  7.2 50.3 %copy-start = (f32[128,128]{1,0:T(8,128)S(1)}, f32[128,128]{1,0:T(8,128)}, u32[]{:S(2)}) copy-start(f32[128,128]{1,0:T(8,128)} %param.7) | copy-start | bytes 196612
  7.2 53.8 %all-gather.3.cloned.1.call-start = ((), (), s32[]{:S(2)}) async-start(), calls=%async_computation | async-start | bytes 1081344 | tf_op jit(solution)/shard_map/all_gather | solution.py:43
  7.9 179.3 %all-reduce.3.cloned.1.call-start = ((), (), s32[]{:S(2)}) async-start(), calls=%async_computation.1 | async-start | bytes 131072 | tf_op jit(solution)/shard_map/psum | solution.py:12
  61.0 48.2 %copy-start.1 = (bf16[4096,128]{1,0:T(8,128)(2,1)S(1)}, bf16[4096,128]{1,0:T(8,128)(2,1)}, u32[]{:S(2)}) copy-start(bf16[4096,128]{1,0:T(8,128)(2,1)} %all-gather.3.cloned.1.call-done) | copy-start | bytes 3145732
  118.3 177.0 %all-reduce.5.cloned.1.call-start = ((), (), s32[]{:S(2)}) async-start(), calls=%async_computation.2 | async-start | bytes 131072 | tf_op jit(solution)/shard_map/psum | solution.py:12
  652.3 139.3 %copy-start.3 = (f32[1024]{0:T(1024)}, f32[1024]{0:T(1024)S(1)}, u32[]{:S(2)}) copy-start(f32[1024]{0:T(1024)S(1)} %add_subtract_fusion.1) | copy-start | bytes 12292
  652.3 263.7 %copy-start.2 = (f32[128,128]{0,1:T(8,128)S(1)}, f32[128,128]{0,1:T(8,128)}, u32[]{:S(2)}) copy-start(f32[128,128]{0,1:T(8,128)} %all-reduce.5.cloned.1.call-done) | copy-start | bytes 196612
Sparse Core Ops, SparseCore 0:
  10.6 50.3 all-gather.2
  118.4 68.7 all-reduce.2
  190.8 104.4 all-reduce.4
